TPU v7x, 32 devices: a whole 2x2x4 slice. The times are simulated.
32 devices in a mesh: dp: 8 (over y, x, core), tensor: 4 (over z).
Axes of the slice: x: 2, y: 2, z: 4, core: 2. Of those that a mesh axis runs over, the one named last changes fastest.
Arguments:
- tokens: bfloat16 [4096, 768], P(('dp', 'tensor')), may hold values from -2.5 to 2.5
- condition: bfloat16 [8, 768], P('dp'), may hold values from -2.5 to 2.5
- modulate_weight: bfloat16 [768, 4608], P(None, 'tensor'), may hold values from -0.21875 to 0.21875
- modulate_bias: float32 [4608], P('tensor'), may hold values from -0.75 to 0.75
- heads_weight: bfloat16 [3, 768, 768], P(None, None, 'tensor'), may hold values from -0.21875 to 0.21875
- heads_bias: float32 [2, 768], P(None, 'tensor'), may hold values from -0.75 to 0.75
- output_weight: bfloat16 [768, 768], P('tensor'), may hold values from -0.875 to 0.875
- output_bias: float32 [768], replicated, may hold values from -0.75 to 0.75
- first_weight: bfloat16 [768, 3072], P(None, 'tensor'), may hold values from -0.21875 to 0.21875
- first_bias: float32 [3072], P('tensor'), may hold values from -0.75 to 0.75
- second_weight: bfloat16 [3072, 768], P('tensor'), may hold values from -0.109375 to 0.109375
- second_bias: float32 [768], replicated, may hold values from -0.75 to 0.75
- cotangent: bfloat16 [4096, 768], P(('dp', 'tensor')), may hold values from -2.5 to 2.5
Outputs:
- output: bfloat16 [4096, 768], P(('dp', 'tensor'))
- token_grad: float32 [4096, 768], P(('dp', 'tensor'))
- modulate_weight_grad: float32 [768, 4608], P('dp', 'tensor')
- modulate_bias_grad: float32 [4608], P('tensor')
- heads_weight_grad: float32 [3, 768, 768], P(None, 'dp', 'tensor')
- heads_bias_grad: float32 [2, 768], P(None, 'tensor')
- output_weight_grad: float32 [768, 768], P('tensor', 'dp')
- output_bias_grad: float32 [768], replicated
- first_weight_grad: float32 [768, 3072], P('dp', 'tensor')
- first_bias_grad: float32 [3072], P('tensor')
- second_weight_grad: float32 [3072, 768], P('tensor', 'dp')
- second_bias_grad: float32 [768], replicated
All inputs are finite; a program needn't handle non-finite values.
Results may differ from a plain program's by a relative error of at most 0.012.
The roundings to bfloat16 on the way count: a program that leaves them out, or rounds other values in their place, can miss the bound.
Values may be sent and summed in bfloat16 or wider, within the bound.
A program may use at most 128 MiB of HBM per device.

v0:
```python
from functools import partial
import jax
import jax.numpy as jnp
from jax import lax
from jax.sharding import PartitionSpec as P

HD = 64
LEN = 512
EPSILON = 1e-06
HIGHEST_PRECISION = lax.Precision.HIGHEST


def layer_norm(values):
    centred = values - jnp.mean(values, axis=-1, keepdims=True)
    inverse = lax.rsqrt(jnp.mean(centred * centred, axis=-1, keepdims=True) + EPSILON)
    return (centred * inverse, inverse)


def norm_back(grade, normed, inverse):
    return inverse * (
        grade
        - jnp.mean(grade, axis=-1, keepdims=True)
        - normed * jnp.mean(grade * normed, axis=-1, keepdims=True)
    )


def matmul(left, right):
    return jnp.dot(left, right, preferred_element_type=jnp.float32)


def left_contract(left, right):
    return lax.dot_general(
        left, right, (((0,), (0,)), ((), ())), preferred_element_type=jnp.float32
    )


def right_contract(left, right):
    return lax.dot_general(
        left, right, (((1,), (1,)), ((), ())), preferred_element_type=jnp.float32
    )


def exact_left(left, right):
    return lax.dot_general(
        left,
        right,
        (((0,), (0,)), ((), ())),
        precision=HIGHEST_PRECISION,
        preferred_element_type=jnp.float32,
    )


def head_cols(values, head):
    return values[:, head * HD : (head + 1) * HD]


def attend_forward(blocks):
    query_block, key_block, value_block = blocks
    outputs = []
    sums = []
    for head in range(query_block.shape[1] // HD):
        scores = right_contract(head_cols(query_block, head), head_cols(key_block, head)) * HD ** (
            -0.5
        )
        peak = jnp.max(scores, axis=-1, keepdims=True)
        expo = jnp.exp(scores - peak)
        total = jnp.sum(expo, axis=-1, keepdims=True)
        probability = (expo / total).astype(jnp.bfloat16)
        outputs.append(matmul(probability, head_cols(value_block, head)))
        sums.append((peak + jnp.log(total))[:, 0])
    return (jnp.concatenate(outputs, axis=1).astype(jnp.bfloat16), jnp.stack(sums))


def attend_backward(blocks):
    query_block, key_block, value_block, grade_block, logsum = blocks
    query_parts = []
    key_parts = []
    value_parts = []
    for head in range(query_block.shape[1] // HD):
        query_head = head_cols(query_block, head)
        key_head = head_cols(key_block, head)
        grade_head = head_cols(grade_block, head)
        scores = right_contract(query_head, key_head) * HD ** (-0.5)
        probability = jnp.exp(scores - logsum[head][:, None])
        value_parts.append(left_contract(probability.astype(jnp.bfloat16), grade_head))
        prob_grad = right_contract(grade_head, head_cols(value_block, head))
        score_grad = probability * (
            prob_grad - jnp.sum(probability * prob_grad, axis=-1, keepdims=True)
        )
        score_low = score_grad.astype(jnp.bfloat16)
        query_parts.append(matmul(score_low, key_head) * HD ** (-0.5))
        key_parts.append(left_contract(score_low, query_head) * HD ** (-0.5))
    return jnp.stack(
        [
            jnp.concatenate(query_parts, axis=1),
            jnp.concatenate(key_parts, axis=1),
            jnp.concatenate(value_parts, axis=1),
        ]
    ).astype(jnp.bfloat16)


def local(
    tokens,
    condition,
    modulate_weight,
    modulate_bias,
    heads_weight,
    heads_bias,
    output_weight,
    output_bias,
    first_weight,
    first_bias,
    second_weight,
    second_bias,
    cotangent,
):
    tensor_rank = lax.axis_index("tensor")
    row_count = tokens.shape[0]
    model_width = tokens.shape[1]
    latent_count = condition.shape[0]
    local_width = heads_weight.shape[2]
    group_rows = latent_count * LEN
    silu_cond = jax.nn.silu(condition.astype(jnp.float32)).astype(jnp.bfloat16)
    modulate_local = matmul(silu_cond, modulate_weight) + modulate_bias
    modulation = lax.all_gather(modulate_local, "tensor", axis=1, tiled=True)
    latent_of_row = (tensor_rank * row_count + jnp.arange(row_count, dtype=jnp.int32)) // LEN
    selector = (
        latent_of_row[:, None] == jnp.arange(latent_count, dtype=jnp.int32)[None, :]
    ).astype(jnp.float32)
    row_mods = jnp.dot(selector, modulation, precision=HIGHEST_PRECISION)
    pieces = [row_mods[:, member * model_width : (member + 1) * model_width] for member in range(6)]
    shift_attn, scale_attn, gate_attn, shift_feed, scale_feed, gate_feed = pieces
    residual = tokens.astype(jnp.float32)
    normed_first, inverse_first = layer_norm(residual)
    attention_in = (normed_first * (1.0 + scale_attn) + shift_attn).astype(jnp.bfloat16)
    attention_all = lax.all_gather(attention_in, "tensor", axis=0, tiled=True)
    projected = jnp.einsum(
        "td,sde->ste", attention_all, heads_weight, preferred_element_type=jnp.float32
    )
    query_rows = (projected[0] + heads_bias[0]).astype(jnp.bfloat16)
    key_rows = projected[1].astype(jnp.bfloat16)
    value_rows = (projected[2] + heads_bias[1]).astype(jnp.bfloat16)
    shaped = (latent_count, LEN, local_width)
    query_blocks = query_rows.reshape(shaped)
    key_blocks = key_rows.reshape(shaped)
    value_blocks = value_rows.reshape(shaped)
    mixture, logsum = lax.map(attend_forward, (query_blocks, key_blocks, value_blocks))
    mixture = mixture.reshape(group_rows, local_width)
    branch_attn = (
        lax.psum_scatter(
            matmul(
                lax.slice_in_dim(mixture, 0, lax.axis_size("tensor") * row_count, axis=0),
                output_weight,
            ),
            "tensor",
            scatter_dimension=0,
            tiled=True,
        )
        + output_bias
    )
    residual_mid = residual + gate_attn * branch_attn
    normed_second, inverse_second = layer_norm(residual_mid)
    feed_in = (normed_second * (1.0 + scale_feed) + shift_feed).astype(jnp.bfloat16)
    feed_all = lax.all_gather(feed_in, "tensor", axis=0, tiled=True)
    hidden_pre = matmul(feed_all, first_weight) + first_bias
    activated = jax.nn.gelu(hidden_pre, approximate=True).astype(jnp.bfloat16)
    branch_feed = (
        lax.psum_scatter(
            matmul(
                lax.slice_in_dim(activated, 0, lax.axis_size("tensor") * row_count, axis=0),
                second_weight,
            ).astype(jnp.bfloat16),
            "tensor",
            scatter_dimension=0,
            tiled=True,
        ).astype(jnp.float32)
        + second_bias
    )
    output = (residual_mid + gate_feed * branch_feed).astype(jnp.bfloat16)
    tangent = cotangent.astype(jnp.float32)
    feed_grad = (gate_feed * tangent).astype(jnp.bfloat16)
    feed_grad_all = lax.all_gather(feed_grad, "tensor", axis=0, tiled=True)
    grad_second_bias = jnp.sum(feed_grad_all, axis=0, dtype=jnp.float32)
    grad_second_weight = left_contract(activated, feed_grad_all)
    activated_grad = right_contract(feed_grad_all, second_weight)
    unused_value, gelu_back = jax.vjp(partial(jax.nn.gelu, approximate=True), hidden_pre)
    pre_grad = gelu_back(activated_grad)[0].astype(jnp.bfloat16)
    grad_first_bias = jnp.sum(pre_grad, axis=0, dtype=jnp.float32)
    grad_first_weight = left_contract(feed_all, pre_grad)
    feed_in_grad = lax.psum_scatter(
        right_contract(
            lax.slice_in_dim(pre_grad, 0, lax.axis_size("tensor") * row_count, axis=0), first_weight
        ),
        "tensor",
        scatter_dimension=0,
        tiled=True,
    )
    mid_grad = tangent + norm_back(feed_in_grad * (1.0 + scale_feed), normed_second, inverse_second)
    attn_grad = (gate_attn * mid_grad).astype(jnp.bfloat16)
    attn_grad_all = lax.all_gather(attn_grad, "tensor", axis=0, tiled=True)
    grad_output_bias = jnp.sum(attn_grad_all, axis=0, dtype=jnp.float32)
    grad_output_weight = left_contract(mixture, attn_grad_all)
    mixture_grad = right_contract(attn_grad_all, output_weight).astype(jnp.bfloat16)
    stacked_grads = lax.map(
        attend_backward,
        (query_blocks, key_blocks, value_blocks, mixture_grad.reshape(shaped), logsum),
    )
    heads_grad = jnp.swapaxes(stacked_grads, 0, 1).reshape(3, group_rows, local_width)
    grad_heads_weight = jnp.einsum(
        "td,ste->sde", attention_all, heads_grad, preferred_element_type=jnp.float32
    )
    grad_heads_bias = jnp.stack(
        [
            jnp.sum(heads_grad[0], axis=0, dtype=jnp.float32),
            jnp.sum(heads_grad[2], axis=0, dtype=jnp.float32),
        ]
    )
    attn_in_grad = lax.psum_scatter(
        jnp.einsum("ste,sde->td", heads_grad, heads_weight, preferred_element_type=jnp.float32),
        "tensor",
        scatter_dimension=0,
        tiled=True,
    )
    token_grad = mid_grad + norm_back(
        attn_in_grad * (1.0 + scale_attn), normed_first, inverse_first
    )
    row_terms = jnp.concatenate(
        [
            attn_in_grad,
            attn_in_grad * normed_first,
            mid_grad * branch_attn,
            feed_in_grad,
            feed_in_grad * normed_second,
            tangent * branch_feed,
        ],
        axis=1,
    )
    modulation_partial = exact_left(selector, row_terms)
    modulation_grad = lax.psum_scatter(
        modulation_partial, "tensor", scatter_dimension=1, tiled=True
    )
    grad_modulate_bias = jnp.sum(modulation_grad, axis=0)
    bias_total = lax.psum(
        (grad_modulate_bias, grad_heads_bias, grad_output_bias, grad_first_bias, grad_second_bias),
        "dp",
    )
    cond_all, modulation_all = (
        lax.all_gather(silu_cond.astype(jnp.float32), "dp", axis=0, tiled=True),
        lax.all_gather(modulation_grad, "dp", axis=0, tiled=True),
    )
    share = model_width // lax.axis_size("dp")
    cond_share = lax.dynamic_slice_in_dim(cond_all, lax.axis_index("dp") * share, share, 1)
    grad_modulate_weight = exact_left(cond_share, modulation_all)
    matrices = (
        lax.psum_scatter(grad_heads_weight, "dp", scatter_dimension=1, tiled=True),
        lax.psum_scatter(grad_output_weight, "dp", scatter_dimension=1, tiled=True),
        lax.psum_scatter(grad_first_weight, "dp", scatter_dimension=0, tiled=True),
        lax.psum_scatter(grad_second_weight, "dp", scatter_dimension=1, tiled=True),
    )
    return (
        output,
        token_grad,
        grad_modulate_weight,
        bias_total[0],
        matrices[0],
        bias_total[1],
        matrices[1],
        bias_total[2],
        matrices[2],
        bias_total[3],
        matrices[3],
        bias_total[4],
    )


def solution(mesh):
    in_specs = (
        P(("dp", "tensor"), None),
        P("dp", None),
        P(None, "tensor"),
        P("tensor"),
        P(None, None, "tensor"),
        P(None, "tensor"),
        P("tensor", None),
        P(),
        P(None, "tensor"),
        P("tensor"),
        P("tensor", None),
        P(),
        P(("dp", "tensor"), None),
    )
    out_specs = (
        P(("dp", "tensor"), None),
        P(("dp", "tensor"), None),
        P("dp", "tensor"),
        P("tensor"),
        P(None, "dp", "tensor"),
        P(None, "tensor"),
        P("tensor", "dp"),
        P(),
        P("dp", "tensor"),
        P("tensor"),
        P("tensor", "dp"),
        P(),
    )
    return jax.shard_map(local, mesh=mesh, in_specs=in_specs, out_specs=out_specs, check_vma=False)
```

profile of v0, /device:TPU:0, one launch (start us, length us, event | category | flops | bytes accessed | tf_op | source)
XLA Modules:
  0.0 488.1 jit_solution(5927712620343426322)
XLA Ops:
  11.4 14.9 %all-gather.1 = f32[4,1,1152]{2,1,0:T(1,128)S(1)} all-gather(f32[1,1,1152]{2,1,0:T(1,128)S(1)} %reshape.153), channel_id=2, replica_groups=mesh['dp'=8,'tensor'=4] {'tensor'}, dimensions={0}, use_global_device_ids=true | all-gather | bytes 23040 | tf_op jit(solution)/shard_map/all_gather | solution.py:125
  27.0 17.7 %all_gather.22 = bf16[512,768]{1,0:T(8,128)(2,1)S(1)} all-gather(bf16[128,768]{1,0:T(8,128)(2,1)S(1)} %fusion.33), channel_id=1, replica_groups=mesh['dp'=8,'tensor'=4] {'tensor'}, dimensions={0}, use_global_device_ids=true | all-gather | bytes 983040 | tf_op jit(solution)/shard_map/all_gather | solution.py:136
  49.6 1.6 fusion.50
  51.3 35.5 %reduce-scatter.16.cloned.1.call-done = f32[128,768]{1,0:T(8,128)} async-done(((f32[512,768]{1,0:T(8,128)}), f32[128,768]{1,0:T(8,128)}) %reduce-scatter.16.cloned.1.call-update) | async-done | bytes 393232 | tf_op jit(solution)/shard_map/reduce_scatter | solution.py:150
  88.3 1.6 fusion.40
  89.9 18.1 %all_gather.24 = bf16[512,768]{1,0:T(8,128)(2,1)S(1)} all-gather(bf16[128,768]{1,0:T(8,128)(2,1)S(1)} %get-tuple-element.91), channel_id=1, replica_groups=mesh['dp'=8,'tensor'=4] {'tensor'}, dimensions={0}, use_global_device_ids=true | all-gather | bytes 983040 | tf_op jit(solution)/shard_map/all_gather | solution.py:182
  108.0 17.5 %all_gather.23 = bf16[512,768]{1,0:T(8,128)(2,1)S(1)} all-gather(bf16[128,768]{1,0:T(8,128)(2,1)S(1)} %get-tuple-element.92), channel_id=1, replica_groups=mesh['dp'=8,'tensor'=4] {'tensor'}, dimensions={0}, use_global_device_ids=true | all-gather | bytes 983040 | tf_op jit(solution)/shard_map/all_gather | solution.py:164
  127.1 3.4 convert_reduce_fusion.1
  131.4 2.0 fusion.106
  133.5 3.8 convolution_convert_fusion
  138.7 29.7 %reduce-scatter.20.cloned.1.call-done = f32[128,768]{1,0:T(8,128)} async-done(((f32[512,768]{1,0:T(8,128)}), f32[128,768]{1,0:T(8,128)}) %reduce-scatter.20.cloned.1.call-update) | async-done | bytes 393232 | tf_op jit(solution)/shard_map/reduce_scatter | solution.py:190
  170.3 22.8 %reduce-scatter.18.cloned.1.call-done = bf16[128,768]{1,0:T(8,128)(2,1)} async-done(((bf16[512,768]{1,0:T(8,128)(2,1)}), bf16[128,768]{1,0:T(8,128)(2,1)}) %reduce-scatter.18.cloned.1.call-update) | async-done | bytes 196624 | tf_op jit(solution)/shard_map/reduce_scatter | solution.py:168
  193.1 2.5 multiply_convert_fusion.4
  195.7 18.3 %all_gather.25 = bf16[512,768]{1,0:T(8,128)(2,1)S(1)} all-gather(bf16[128,768]{1,0:T(8,128)(2,1)S(1)} %get-tuple-element.86), channel_id=1, replica_groups=mesh['dp'=8,'tensor'=4] {'tensor'}, dimensions={0}, use_global_device_ids=true | all-gather | bytes 983040 | tf_op jit(solution)/shard_map/all_gather | solution.py:200
  220.9 2.0 convolution_bitcast_fusion.2
  225.6 3.2 convolution_bitcast_fusion.1
  228.8 4.2 copy.29
  233.0 4.7 reshape.172
  237.8 19.9 %reduce-scatter.22.cloned.1.call-done = f32[128,768]{1,0:T(8,128)} async-done(((f32[512,768]{1,0:T(8,128)}), f32[128,768]{1,0:T(8,128)}) %reduce-scatter.22.cloned.1.call-update) | async-done | bytes 393232 | tf_op jit(solution)/shard_map/reduce_scatter | solution.py:218
  259.1 2.0 fusion.38
  262.2 3.5 convolution_bitcast_fusion
  265.8 4.2 fusion.97
  270.1 3.6 fusion.107
  274.3 9.2 %all-gather.2 = f32[8,1,768]{2,1,0:T(1,128)S(1)} all-gather(f32[1,1,768]{2,1,0:T(1,128)S(1)} %bitcast_convert_fusion), channel_id=1, replica_groups=mesh['dp'=8,'tensor'=4] {'dp'}, dimensions={0}, use_global_device_ids=true | all-gather | bytes 27648 | tf_op jit(solution)/shard_map/all_gather | solution.py:248
  285.4 9.2 %reduce-scatter.32.cloned.1.call-done = f32[96,192]{1,0:T(8,128)} async-done(((f32[768,192]{1,0:T(8,128)}), f32[96,192]{1,0:T(8,128)}) %reduce-scatter.32.cloned.1.call-update) | async-done | bytes 73744
  294.6 1.6 copy.32
  296.3 42.0 %reduce-scatter.30.cloned.1.call-done = f32[96,576]{1,0:T(8,128)} async-done(((f32[768,576]{1,0:T(8,128)}), f32[96,576]{1,0:T(8,128)}) %reduce-scatter.30.cloned.1.call-update) | async-done | bytes 221200
  340.1 48.6 %reduce-scatter.28.cloned.1.call-done = f32[1152,1]{1,0:T(8,128)} async-done(((f32[4608,1]{1,0:T(8,128)}), f32[1152,1]{1,0:T(8,128)}) %reduce-scatter.28.cloned.1.call-update) | async-done | bytes 4624
  391.3 24.4 %all-reduce = (f32[1152]{0:T(1024)}, f32[2,192]{1,0:T(2,128)}, f32[768]{0:T(1024)}, f32[768]{0:T(1024)}, f32[768]{0:T(1024)}) all-reduce(f32[1152]{0:T(1024)S(1)} %bitcast_reduce_fusion, f32[2,192]{1,0:T(2,128)S(1)} %pad_maximum_fusion.6, f32[768]{0:T(1024)S(1)} %convert_reduce_fusion.2, ...), channel_id=1, replica_groups=mesh['dp'=8,'tensor'=4] {'dp'}, use_global_device_ids=true, to_apply=%region_22.23 | all-reduce | flops 3840 | bytes 30720 | tf_op jit(solution)/shard_map/psum | solution.py:243
  415.7 8.1 %all-gather.3 = f32[8,1,1152]{2,1,0:T(1,128)S(1)} all-gather(f32[1,1,1152]{2,1,0:T(1,128)S(1)} %bitcast.98), channel_id=1, replica_groups=mesh['dp'=8,'tensor'=4] {'dp'}, dimensions={0}, use_global_device_ids=true | all-gather | bytes 41472 | tf_op jit(solution)/shard_map/all_gather | solution.py:249
  425.2 10.0 %reduce-scatter.26.cloned.1.call-done = f32[768,96]{0,1:T(8,128)} async-done(((f32[768,768]{0,1:T(8,128)}), f32[768,96]{0,1:T(8,128)}) %reduce-scatter.26.cloned.1.call-update) | async-done | bytes 294928 | tf_op jit(solution)/shard_map/reduce_scatter | solution.py:258
  435.1 46.5 %reduce-scatter.24.cloned.1.call-done = f32[96,768]{1,0:T(8,128)} async-done(((f32[768,768]{1,0:T(8,128)}), f32[96,768]{1,0:T(8,128)}) %reduce-scatter.24.cloned.1.call-update) | async-done | bytes 294928 | tf_op jit(solution)/shard_map/reduce_scatter | solution.py:257
  (226 shorter events, 37.0 us)
Async XLA Ops:
  7.2 79.6 %reduce-scatter.16.cloned.1.call-start = ((), (), s32[]{:S(2)}) async-start(), calls=%async_computation.9 | async-start | bytes 1966080 | tf_op jit(solution)/shard_map/reduce_scatter | solution.py:150
  8.4 18.3 %copy-start.52 = (f32[128]{0:T(128)}, f32[128]{0:T(128)S(1)}, u32[]{:S(2)}) copy-start(f32[128]{0:T(128)S(1)} %broadcast_multiply_fusion.6) | copy-start | bytes 1540
  9.6 17.2 %copy-start.61 = (f32[128]{0:T(128)}, f32[128]{0:T(128)S(1)}, u32[]{:S(2)}) copy-start(f32[128]{0:T(128)S(1)} %add_rsqrt_fusion.1) | copy-start | bytes 1540
  11.4 15.4 %copy-start.8 = (bf16[128,768]{1,0:T(8,128)(2,1)S(1)}, bf16[128,768]{1,0:T(8,128)(2,1)}, u32[]{:S(2)}) copy-start(bf16[128,768]{1,0:T(8,128)(2,1)} %param.13) | copy-start | bytes 589828
  26.8 18.6 %copy-start.5 = (f32[128,4608]{1,0:T(8,128)}, f32[128,4608]{1,0:T(8,128)S(1)}, u32[]{:S(2)}) copy-start(f32[128,4608]{1,0:T(8,128)S(1)} %broadcast_multiply_fusion) | copy-start | bytes 7077892
  26.8 18.0 %copy-start.23 = (bf16[3,768,192]{1,2,0:T(8,128)(2,1)S(1)}, bf16[3,768,192]{1,2,0:T(8,128)(2,1)}, u32[]{:S(2)}) copy-start(bf16[3,768,192]{1,2,0:T(8,128)(2,1)} %param.17) | copy-start | bytes 2654212
  49.6 37.1 %copy-start.46 = (f32[768]{0:T(1024)S(1)}, f32[768]{0:T(1024)}, u32[]{:S(2)}) copy-start(f32[768]{0:T(1024)} %param.20) | copy-start | bytes 9220
  51.2 117.2 %reduce-scatter.20.cloned.1.call-start = ((), (), s32[]{:S(2)}) async-start(), calls=%async_computation.11 | async-start | bytes 1966080 | tf_op jit(solution)/shard_map/reduce_scatter | solution.py:190
  88.0 20.0 %copy-start.49 = (f32[128]{0:T(128)}, f32[128]{0:T(128)S(1)}, u32[]{:S(2)}) copy-start(f32[128]{0:T(128)S(1)} %broadcast_multiply_fusion.5) | copy-start | bytes 1540
  88.2 19.8 %copy-start.59 = (f32[128]{0:T(128)}, f32[128]{0:T(128)S(1)}, u32[]{:S(2)}) copy-start(f32[128]{0:T(128)S(1)} %add_rsqrt_fusion) | copy-start | bytes 1540
  88.3 37.3 %copy-start.65 = (bf16[768,768]{1,0:T(8,128)(2,1)S(1)}, bf16[768,768]{1,0:T(8,128)(2,1)}, u32[]{:S(2)}) copy-start(bf16[768,768]{1,0:T(8,128)(2,1)} %param.23) | copy-start | bytes 3538948
  108.0 17.5 %copy-start.12 = (bf16[512,768]{1,0:T(8,128)(2,1)}, bf16[512,768]{1,0:T(8,128)(2,1)S(1)}, u32[]{:S(2)}) copy-start(bf16[512,768]{1,0:T(8,128)(2,1)S(1)} %all_gather.24) | copy-start | bytes 2359300
  133.4 59.7 %reduce-scatter.18.cloned.1.call-start = ((), (), s32[]{:S(2)}) async-start(), calls=%async_computation.10 | async-start | bytes 983040 | tf_op jit(solution)/shard_map/reduce_scatter | solution.py:168
  137.3 120.4 %reduce-scatter.22.cloned.1.call-start = ((), (), s32[]{:S(2)}) async-start(), calls=%async_computation.12 | async-start | bytes 1966080 | tf_op jit(solution)/shard_map/reduce_scatter | solution.py:218
  193.1 20.8 %copy-start.22 = (bf16[192,768]{1,0:T(8,128)(2,1)S(1)}, bf16[192,768]{1,0:T(8,128)(2,1)}, u32[]{:S(2)}) copy-start(bf16[192,768]{1,0:T(8,128)(2,1)} %param.19) | copy-start | bytes 884740
  195.7 18.7 %copy-start.4 = (f32[512,512]{0,1:T(8,128)S(1)}, f32[512,512]{0,1:T(8,128)}, u32[]{:S(2)}) copy-start(f32[512,512]{0,1:T(8,128)} %copy-done.3) | copy-start | bytes 3145732
  195.7 19.0 %copy-start.26 = (bf16[512,192]{0,1:T(8,128)(2,1)S(1)}, bf16[512,192]{0,1:T(8,128)(2,1)}, u32[]{:S(2)}) copy-start(bf16[512,192]{0,1:T(8,128)(2,1)} %copy-done.25) | copy-start | bytes 589828
  223.0 71.7 %reduce-scatter.32.cloned.1.call-start = ((), (), s32[]{:S(2)}) async-start(), calls=%async_computation.17 | async-start | bytes 884736
  225.5 112.7 %reduce-scatter.30.cloned.1.call-start = ((), (), s32[]{:S(2)}) async-start(), calls=%async_computation.16 | async-start | bytes 2211840
  237.7 20.0 %copy-start.53 = (f32[128]{0:T(128)S(1)}, f32[128]{0:T(128)}, u32[]{:S(2)}) copy-start(f32[128]{0:T(128)} %copy-done.52) | copy-start | bytes 1540
  237.7 20.0 %copy-start.62 = (f32[128]{0:T(128)S(1)}, f32[128]{0:T(128)}, u32[]{:S(2)}) copy-start(f32[128]{0:T(128)} %copy-done.61) | copy-start | bytes 1540
  237.7 21.4 %copy-start.11 = (f32[128,768]{1,0:T(8,128)S(1)}, f32[128,768]{1,0:T(8,128)}, u32[]{:S(2)}) copy-start(f32[128,768]{1,0:T(8,128)} %get-tuple-element.87) | copy-start | bytes 1179652
  237.7 23.4 %copy-start.47 = (f32[768]{0:T(1024)S(1)}, f32[768]{0:T(1024)}, u32[]{:S(2)}) copy-start(f32[768]{0:T(1024)} %param.20) | copy-start | bytes 9220
  237.7 151.0 %reduce-scatter.28.cloned.1.call-start = ((), (), s32[]{:S(2)}) async-start(), calls=%async_computation.15 | async-start | bytes 2949120
  265.7 169.4 %reduce-scatter.26.cloned.1.call-start = ((), (), s32[]{:S(2)}) async-start(), calls=%async_computation.14 | async-start | bytes 2654208 | tf_op jit(solution)/shard_map/reduce_scatter | solution.py:258
  270.0 211.6 %reduce-scatter.24.cloned.1.call-start = ((), (), s32[]{:S(2)}) async-start(), calls=%async_computation.13 | async-start | bytes 2654208 | tf_op jit(solution)/shard_map/reduce_scatter | solution.py:257
  273.6 11.3 %copy-start.34 = (bf16[512,64]{0,1:T(8,128)(2,1)S(1)}, bf16[512,64]{0,1:T(8,128)(2,1)}, u32[]{:S(2)}) copy-start(bf16[512,64]{0,1:T(8,128)(2,1)} %copy-done.33) | copy-start | bytes 196612
  273.6 11.3 %copy-start.38 = (bf16[512,64]{0,1:T(8,128)(2,1)S(1)}, bf16[512,64]{0,1:T(8,128)(2,1)}, u32[]{:S(2)}) copy-start(bf16[512,64]{0,1:T(8,128)(2,1)} %copy-done.37) | copy-start | bytes 196612
  273.7 11.4 %copy-start.32 = (bf16[512,64]{0,1:T(8,128)(2,1)S(1)}, bf16[512,64]{0,1:T(8,128)(2,1)}, u32[]{:S(2)}) copy-start(bf16[512,64]{0,1:T(8,128)(2,1)} %copy-done.31) | copy-start | bytes 196612
  273.7 11.4 %copy-start.36 = (bf16[512,64]{0,1:T(8,128)(2,1)S(1)}, bf16[512,64]{0,1:T(8,128)(2,1)}, u32[]{:S(2)}) copy-start(bf16[512,64]{0,1:T(8,128)(2,1)} %copy-done.35) | copy-start | bytes 196612
  273.7 11.4 %copy-start.40 = (bf16[512,64]{0,1:T(8,128)(2,1)S(1)}, bf16[512,64]{0,1:T(8,128)(2,1)}, u32[]{:S(2)}) copy-start(bf16[512,64]{0,1:T(8,128)(2,1)} %copy-done.39) | copy-start | bytes 196612
  285.2 106.0 %copy-start.63 = (f32[768]{0:T(1024)S(1)}, f32[768]{0:T(1024)}, u32[]{:S(2)}) copy-start(f32[768]{0:T(1024)} %get-tuple-element.84) | copy-start | bytes 9220
  (44 other events, 81.1 us)
Sparse Core Ops, SparseCore 0:
  51.3 35.3 reduce-scatter.15
  133.5 34.8 reduce-scatter.19
  170.8 22.3 reduce-scatter.17
  223.1 34.5 reduce-scatter.21
  260.6 33.9 reduce-scatter.31
  297.9 40.2 reduce-scatter.29
  340.6 47.9 reduce-scatter.27
  393.0 42.1 reduce-scatter.25
  439.1 42.4 reduce-scatter.23
where the time goes:
time: 489 us; the launch traced here: 488 us
  waiting for transfers between devices  264 us (54%)
  blocking collectives  128 us (26%)
  matrix products  38.3 us (8%)
  local copies, waits for them, and re-layouts  23.5 us (5%)
  other arithmetic  18.5 us (4%)
  between operations  14.8 us (3%)
    unnamed x12, waiting for transfers between devices  99.9 us
    reduce_scatter x1, waiting for transfers between devices, local(): lax.psum_scatter(grad_first_weight, 'dp', scatter_dimension=0, tiled=True)  46.5 us
    reduce_scatter x1, waiting for transfers between devices, local(): lax.psum_scatter(matmul(lax.slice_in_dim(mixture, 0, lax.axis_size('tenso...  35.5 us
    reduce_scatter x1, waiting for transfers between devices, local(): lax.psum_scatter(right_contract(lax.slice_in_dim(pre_grad, 0, lax.axis_si...  29.7 us
    psum x1, blocking collectives, local(): lax.psum((grad_modulate_bias, grad_heads_bias, grad_output_bias, grad_fir...  24.4 us
    reduce_scatter x1, waiting for transfers between devices, local(): lax.psum_scatter(matmul(lax.slice_in_dim(activated, 0, lax.axis_size('ten...  22.8 us
    unnamed x143, local copies, waits for them, and re-layouts  21.3 us
    reduce_scatter x1, waiting for transfers between devices, local(): lax.psum_scatter(jnp.einsum('ste,sde->td', heads_grad, heads_weight, pref...  19.9 us
  transfers between devices with their start and end apart: 9, of which 9 were waited for; matrix products, arithmetic and copies ran while one was open for 9% of the time, Pallas kernels for 0%

commit v1 on v0

--- a/solution.py
+++ b/solution.py
@@ -161,7 +161,10 @@
     residual_mid = residual + gate_attn * branch_attn
     normed_second, inverse_second = layer_norm(residual_mid)
     feed_in = (normed_second * (1.0 + scale_feed) + shift_feed).astype(jnp.bfloat16)
-    feed_all = lax.all_gather(feed_in, "tensor", axis=0, tiled=True)
+    _build_floor = lambda sample: jnp.concatenate(
+        lax.all_to_all(jnp.stack(lax.psum(1, "tensor") * [sample], axis=0), "tensor", 0, 0), axis=0
+    )
+    feed_all = _build_floor(feed_in)
     hidden_pre = matmul(feed_all, first_weight) + first_bias
     activated = jax.nn.gelu(hidden_pre, approximate=True).astype(jnp.bfloat16)
     branch_feed = (

time: 489 us -> 499 us (1.020)
    all_gather x1 -> x0, blocking collectives: 17.5 us -> none  [local(): feed_all = lax.all_gather(feed_in, 'tensor', axis=0, tiled=True)]
    all_gather x1, blocking collectives: 18.1 us -> 33.7 us  [local(): feed_grad_all = lax.all_gather(feed_grad, 'tensor', axis=0, tiled=True)]
    unnamed x143 -> x139, local copies, waits for them, and re-layouts: 21.3 us -> 21.7 us
  transfers between devices with their start and end apart: 9 -> 10, of which waited for: 9 -> 9; matrix products, arithmetic and copies ran while one was open for 9% -> 10% of each run, Pallas kernels for 0% -> 0%
where the time goes in v1:
time: 499 us; the launch traced here: 498 us
  waiting for transfers between devices  265 us (53%)
  blocking collectives  126 us (25%)
  matrix products  42.9 us (9%)
  local copies, waits for them, and re-layouts  24.8 us (5%)
  other arithmetic  19.1 us (4%)
  between operations  14.7 us (3%)
    unnamed x12, waiting for transfers between devices  99.9 us
    reduce_scatter x1, waiting for transfers between devices, local(): lax.psum_scatter(grad_first_weight, 'dp', scatter_dimension=0, tiled=True)  46.5 us
    reduce_scatter x1, waiting for transfers between devices, local(): lax.psum_scatter(matmul(lax.slice_in_dim(mixture, 0, lax.axis_size('tenso...  35.6 us
    all_gather x1, blocking collectives, local(): feed_grad_all = lax.all_gather(feed_grad, 'tensor', axis=0, tiled=True)  33.7 us
    reduce_scatter x1, waiting for transfers between devices, local(): lax.psum_scatter(right_contract(lax.slice_in_dim(pre_grad, 0, lax.axis_si...  30.5 us
    psum x1, blocking collectives, local(): lax.psum((grad_modulate_bias, grad_heads_bias, grad_output_bias, grad_fir...  24.4 us
    reduce_scatter x1, waiting for transfers between devices, local(): lax.psum_scatter(matmul(lax.slice_in_dim(activated, 0, lax.axis_size('ten...  22.8 us
    unnamed x139, local copies, waits for them, and re-layouts  21.7 us
  transfers between devices with their start and end apart: 10, of which 9 were waited for; matrix products, arithmetic and copies ran while one was open for 10% of the time, Pallas kernels for 0%

profile of v1, /device:TPU:0, one launch (start us, length us, event | category | flops | bytes accessed | tf_op | source)
XLA Modules:
  0.0 497.7 jit_solution(11279027960275689916)
XLA Ops:
  11.4 14.9 %all-gather.1 = f32[4,1,1152]{2,1,0:T(1,128)S(1)} all-gather(f32[1,1,1152]{2,1,0:T(1,128)S(1)} %reshape.159), channel_id=2, replica_groups=mesh['dp'=8,'tensor'=4] {'tensor'}, dimensions={0}, use_global_device_ids=true | all-gather | bytes 23040 | tf_op jit(solution)/shard_map/all_gather | solution.py:125
  27.0 17.7 %all_gather.19 = bf16[512,768]{1,0:T(8,128)(2,1)S(1)} all-gather(bf16[128,768]{1,0:T(8,128)(2,1)S(1)} %fusion.33), channel_id=1, replica_groups=mesh['dp'=8,'tensor'=4] {'tensor'}, dimensions={0}, use_global_device_ids=true | all-gather | bytes 983040 | tf_op jit(solution)/shard_map/all_gather | solution.py:136
  51.5 35.6 %reduce-scatter.16.cloned.1.call-done = f32[128,768]{1,0:T(8,128)} async-done(((f32[512,768]{1,0:T(8,128)}), f32[128,768]{1,0:T(8,128)}) %reduce-scatter.16.cloned.1.call-update) | async-done | bytes 393232 | tf_op jit(solution)/shard_map/reduce_scatter | solution.py:150
  88.5 2.2 fusion.40
  91.7 4.2 all-to-all-start
  95.9 33.7 %all_gather.20 = bf16[512,768]{1,0:T(8,128)(2,1)S(1)} all-gather(bf16[128,768]{1,0:T(8,128)(2,1)} %get-tuple-element.91), channel_id=1, replica_groups=mesh['dp'=8,'tensor'=4] {'tensor'}, dimensions={0}, use_global_device_ids=true | all-gather | bytes 983040 | tf_op jit(solution)/shard_map/all_gather | solution.py:185
  130.5 3.3 fusion.105
  133.8 5.5 %convert_reduce_fusion.1 = (f32[768]{0:T(1024)}, bf16[512,768]{1,0:T(8,128)(2,1)S(1)}, f32[512,768]{1,0:T(8,128)}) fusion(f32[512,768]{1,0:T(8,128)} %fusion.105, f32[768]{0:T(1024)S(1)} %copy-done.64, bf16[512,768]{1,0:T(8,128)(2,1)} %bitcast.10, bf16[768,768]{1,0:T(8,128)(2,1)} %param.21), kind=kOutput, calls=%fused_computation.11 | convolution fusion | flops 613022976 | bytes 5904384 | tf_op jit(solution)/shard_map/dot_general | solution.py:28
  140.2 2.0 fusion.106
  142.3 3.8 convolution_convert_fusion
  147.5 30.5 %reduce-scatter.20.cloned.1.call-done = f32[128,768]{1,0:T(8,128)} async-done(((f32[512,768]{1,0:T(8,128)}), f32[128,768]{1,0:T(8,128)}) %reduce-scatter.20.cloned.1.call-update) | async-done | bytes 393232 | tf_op jit(solution)/shard_map/reduce_scatter | solution.py:193
  179.9 22.8 %reduce-scatter.18.cloned.1.call-done = bf16[128,768]{1,0:T(8,128)(2,1)} async-done(((bf16[512,768]{1,0:T(8,128)(2,1)}), bf16[128,768]{1,0:T(8,128)(2,1)}) %reduce-scatter.18.cloned.1.call-update) | async-done | bytes 196624 | tf_op jit(solution)/shard_map/reduce_scatter | solution.py:171
  202.7 2.5 multiply_convert_fusion.4
  205.2 18.3 %all_gather.21 = bf16[512,768]{1,0:T(8,128)(2,1)S(1)} all-gather(bf16[128,768]{1,0:T(8,128)(2,1)S(1)} %get-tuple-element.86), channel_id=1, replica_groups=mesh['dp'=8,'tensor'=4] {'tensor'}, dimensions={0}, use_global_device_ids=true | all-gather | bytes 983040 | tf_op jit(solution)/shard_map/all_gather | solution.py:203
  230.5 2.0 convolution_bitcast_fusion.2
  235.2 3.2 convolution_bitcast_fusion.1
  238.3 4.2 copy.29
  242.6 4.7 reshape.178
  247.3 19.9 %reduce-scatter.22.cloned.1.call-done = f32[128,768]{1,0:T(8,128)} async-done(((f32[512,768]{1,0:T(8,128)}), f32[128,768]{1,0:T(8,128)}) %reduce-scatter.22.cloned.1.call-update) | async-done | bytes 393232 | tf_op jit(solution)/shard_map/reduce_scatter | solution.py:221
  268.7 2.0 fusion.38
  271.8 3.5 convolution_bitcast_fusion
  275.3 4.2 fusion.97
  279.6 3.6 fusion.107
  283.9 9.2 %all-gather.2 = f32[8,1,768]{2,1,0:T(1,128)S(1)} all-gather(f32[1,1,768]{2,1,0:T(1,128)S(1)} %bitcast_convert_fusion), channel_id=1, replica_groups=mesh['dp'=8,'tensor'=4] {'dp'}, dimensions={0}, use_global_device_ids=true | all-gather | bytes 27648 | tf_op jit(solution)/shard_map/all_gather | solution.py:251
  295.0 9.2 %reduce-scatter.32.cloned.1.call-done = f32[96,192]{1,0:T(8,128)} async-done(((f32[768,192]{1,0:T(8,128)}), f32[96,192]{1,0:T(8,128)}) %reduce-scatter.32.cloned.1.call-update) | async-done | bytes 73744
  304.2 1.6 copy.32
  305.8 41.9 %reduce-scatter.30.cloned.1.call-done = f32[96,576]{1,0:T(8,128)} async-done(((f32[768,576]{1,0:T(8,128)}), f32[96,576]{1,0:T(8,128)}) %reduce-scatter.30.cloned.1.call-update) | async-done | bytes 221200
  349.7 48.6 %reduce-scatter.28.cloned.1.call-done = f32[1152,1]{1,0:T(8,128)} async-done(((f32[4608,1]{1,0:T(8,128)}), f32[1152,1]{1,0:T(8,128)}) %reduce-scatter.28.cloned.1.call-update) | async-done | bytes 4624
  400.9 24.4 %all-reduce = (f32[1152]{0:T(1024)}, f32[2,192]{1,0:T(2,128)}, f32[768]{0:T(1024)}, f32[768]{0:T(1024)}, f32[768]{0:T(1024)}) all-reduce(f32[1152]{0:T(1024)S(1)} %bitcast_reduce_fusion, f32[2,192]{1,0:T(2,128)S(1)} %pad_maximum_fusion.6, f32[768]{0:T(1024)S(1)} %convert_reduce_fusion.2, ...), channel_id=1, replica_groups=mesh['dp'=8,'tensor'=4] {'dp'}, use_global_device_ids=true, to_apply=%region_22.23 | all-reduce | flops 3840 | bytes 30720 | tf_op jit(solution)/shard_map/psum | solution.py:246
  425.3 8.1 %all-gather.3 = f32[8,1,1152]{2,1,0:T(1,128)S(1)} all-gather(f32[1,1,1152]{2,1,0:T(1,128)S(1)} %bitcast.99), channel_id=1, replica_groups=mesh['dp'=8,'tensor'=4] {'dp'}, dimensions={0}, use_global_device_ids=true | all-gather | bytes 41472 | tf_op jit(solution)/shard_map/all_gather | solution.py:252
  434.7 10.0 %reduce-scatter.26.cloned.1.call-done = f32[768,96]{0,1:T(8,128)} async-done(((f32[768,768]{0,1:T(8,128)}), f32[768,96]{0,1:T(8,128)}) %reduce-scatter.26.cloned.1.call-update) | async-done | bytes 294928 | tf_op jit(solution)/shard_map/reduce_scatter | solution.py:261
  444.7 46.5 %reduce-scatter.24.cloned.1.call-done = f32[96,768]{1,0:T(8,128)} async-done(((f32[768,768]{1,0:T(8,128)}), f32[96,768]{1,0:T(8,128)}) %reduce-scatter.24.cloned.1.call-update) | async-done | bytes 294928 | tf_op jit(solution)/shard_map/reduce_scatter | solution.py:260
  (224 shorter events, 39.1 us)
Async XLA Ops:
  7.2 79.8 %reduce-scatter.16.cloned.1.call-start = ((), (), s32[]{:S(2)}) async-start(), calls=%async_computation.10 | async-start | bytes 1966080 | tf_op jit(solution)/shard_map/reduce_scatter | solution.py:150
  8.4 18.3 %copy-start.51 = (f32[128]{0:T(128)}, f32[128]{0:T(128)S(1)}, u32[]{:S(2)}) copy-start(f32[128]{0:T(128)S(1)} %broadcast_multiply_fusion.6) | copy-start | bytes 1540
  9.6 17.2 %copy-start.60 = (f32[128]{0:T(128)}, f32[128]{0:T(128)S(1)}, u32[]{:S(2)}) copy-start(f32[128]{0:T(128)S(1)} %add_rsqrt_fusion.1) | copy-start | bytes 1540
  11.4 15.4 %copy-start.8 = (bf16[128,768]{1,0:T(8,128)(2,1)S(1)}, bf16[128,768]{1,0:T(8,128)(2,1)}, u32[]{:S(2)}) copy-start(bf16[128,768]{1,0:T(8,128)(2,1)} %param.13) | copy-start | bytes 589828
  26.8 18.6 %copy-start.5 = (f32[128,4608]{1,0:T(8,128)}, f32[128,4608]{1,0:T(8,128)S(1)}, u32[]{:S(2)}) copy-start(f32[128,4608]{1,0:T(8,128)S(1)} %broadcast_multiply_fusion) | copy-start | bytes 7077892
  26.8 18.0 %copy-start.22 = (bf16[3,768,192]{1,2,0:T(8,128)(2,1)S(1)}, bf16[3,768,192]{1,2,0:T(8,128)(2,1)}, u32[]{:S(2)}) copy-start(bf16[3,768,192]{1,2,0:T(8,128)(2,1)} %param.17) | copy-start | bytes 2654212
  49.8 37.2 %copy-start.45 = (f32[768]{0:T(1024)S(1)}, f32[768]{0:T(1024)}, u32[]{:S(2)}) copy-start(f32[768]{0:T(1024)} %param.20) | copy-start | bytes 9220
  91.7 42.1 %all-to-all-start = ((bf16[4,128,768]{2,1,0:T(8,128)(2,1)}), bf16[4,128,768]{2,1,0:T(8,128)(2,1)}, u32[]{:S(2)}, u32[]{:S(2)}) async-start(bf16[4,128,768]{2,1,0:T(8,128)(2,1)} %stack.38), calls=%async_computation.1 | async-start | bytes 1572864 | tf_op jit(solution)/shard_map/all_to_all | solution.py:165
  95.9 82.2 %reduce-scatter.20.cloned.1.call-start = ((), (), s32[]{:S(2)}) async-start(), calls=%async_computation.12 | async-start | bytes 1966080 | tf_op jit(solution)/shard_map/reduce_scatter | solution.py:193
  133.8 6.4 %copy-start.63 = (bf16[768,768]{1,0:T(8,128)(2,1)S(1)}, bf16[768,768]{1,0:T(8,128)(2,1)}, u32[]{:S(2)}) copy-start(bf16[768,768]{1,0:T(8,128)(2,1)} %param.21) | copy-start | bytes 3538948
  142.2 60.5 %reduce-scatter.18.cloned.1.call-start = ((), (), s32[]{:S(2)}) async-start(), calls=%async_computation.11 | async-start | bytes 983040 | tf_op jit(solution)/shard_map/reduce_scatter | solution.py:171
  146.1 121.2 %reduce-scatter.22.cloned.1.call-start = ((), (), s32[]{:S(2)}) async-start(), calls=%async_computation.13 | async-start | bytes 1966080 | tf_op jit(solution)/shard_map/reduce_scatter | solution.py:221
  202.7 20.8 %copy-start.21 = (bf16[192,768]{1,0:T(8,128)(2,1)S(1)}, bf16[192,768]{1,0:T(8,128)(2,1)}, u32[]{:S(2)}) copy-start(bf16[192,768]{1,0:T(8,128)(2,1)} %param.19) | copy-start | bytes 884740
  205.2 18.7 %copy-start.4 = (f32[512,512]{0,1:T(8,128)S(1)}, f32[512,512]{0,1:T(8,128)}, u32[]{:S(2)}) copy-start(f32[512,512]{0,1:T(8,128)} %copy-done.3) | copy-start | bytes 3145732
  205.2 19.0 %copy-start.25 = (bf16[512,192]{0,1:T(8,128)(2,1)S(1)}, bf16[512,192]{0,1:T(8,128)(2,1)}, u32[]{:S(2)}) copy-start(bf16[512,192]{0,1:T(8,128)(2,1)} %copy-done.24) | copy-start | bytes 589828
  224.3 4.8 copy-start.28
  232.5 71.7 %reduce-scatter.32.cloned.1.call-start = ((), (), s32[]{:S(2)}) async-start(), calls=%async_computation.18 | async-start | bytes 884736
  235.1 112.7 %reduce-scatter.30.cloned.1.call-start = ((), (), s32[]{:S(2)}) async-start(), calls=%async_computation.17 | async-start | bytes 2211840
  247.2 20.0 %copy-start.52 = (f32[128]{0:T(128)S(1)}, f32[128]{0:T(128)}, u32[]{:S(2)}) copy-start(f32[128]{0:T(128)} %copy-done.51) | copy-start | bytes 1540
  247.2 20.0 %copy-start.61 = (f32[128]{0:T(128)S(1)}, f32[128]{0:T(128)}, u32[]{:S(2)}) copy-start(f32[128]{0:T(128)} %copy-done.60) | copy-start | bytes 1540
  247.2 21.4 %copy-start.10 = (f32[128,768]{1,0:T(8,128)S(1)}, f32[128,768]{1,0:T(8,128)}, u32[]{:S(2)}) copy-start(f32[128,768]{1,0:T(8,128)} %get-tuple-element.87) | copy-start | bytes 1179652
  247.3 23.4 %copy-start.46 = (f32[768]{0:T(1024)S(1)}, f32[768]{0:T(1024)}, u32[]{:S(2)}) copy-start(f32[768]{0:T(1024)} %param.20) | copy-start | bytes 9220
  247.3 151.0 %reduce-scatter.28.cloned.1.call-start = ((), (), s32[]{:S(2)}) async-start(), calls=%async_computation.16 | async-start | bytes 2949120
  275.3 169.4 %reduce-scatter.26.cloned.1.call-start = ((), (), s32[]{:S(2)}) async-start(), calls=%async_computation.15 | async-start | bytes 2654208 | tf_op jit(solution)/shard_map/reduce_scatter | solution.py:261
  279.6 211.6 %reduce-scatter.24.cloned.1.call-start = ((), (), s32[]{:S(2)}) async-start(), calls=%async_computation.14 | async-start | bytes 2654208 | tf_op jit(solution)/shard_map/reduce_scatter | solution.py:260
  283.2 11.3 %copy-start.29 = (bf16[512,64]{0,1:T(8,128)(2,1)S(1)}, bf16[512,64]{0,1:T(8,128)(2,1)}, u32[]{:S(2)}) copy-start(bf16[512,64]{0,1:T(8,128)(2,1)} %copy-done.28) | copy-start | bytes 196612
  283.2 11.3 %copy-start.33 = (bf16[512,64]{0,1:T(8,128)(2,1)S(1)}, bf16[512,64]{0,1:T(8,128)(2,1)}, u32[]{:S(2)}) copy-start(bf16[512,64]{0,1:T(8,128)(2,1)} %copy-done.32) | copy-start | bytes 196612
  283.2 11.3 %copy-start.37 = (bf16[512,64]{0,1:T(8,128)(2,1)S(1)}, bf16[512,64]{0,1:T(8,128)(2,1)}, u32[]{:S(2)}) copy-start(bf16[512,64]{0,1:T(8,128)(2,1)} %copy-done.36) | copy-start | bytes 196612
  283.2 11.4 %copy-start.31 = (bf16[512,64]{0,1:T(8,128)(2,1)S(1)}, bf16[512,64]{0,1:T(8,128)(2,1)}, u32[]{:S(2)}) copy-start(bf16[512,64]{0,1:T(8,128)(2,1)} %copy-done.30) | copy-start | bytes 196612
  283.2 11.4 %copy-start.35 = (bf16[512,64]{0,1:T(8,128)(2,1)S(1)}, bf16[512,64]{0,1:T(8,128)(2,1)}, u32[]{:S(2)}) copy-start(bf16[512,64]{0,1:T(8,128)(2,1)} %copy-done.34) | copy-start | bytes 196612
  283.3 11.4 %copy-start.39 = (bf16[512,64]{0,1:T(8,128)(2,1)S(1)}, bf16[512,64]{0,1:T(8,128)(2,1)}, u32[]{:S(2)}) copy-start(bf16[512,64]{0,1:T(8,128)(2,1)} %copy-done.38) | copy-start | bytes 196612
  294.8 106.0 %copy-start.62 = (f32[768]{0:T(1024)S(1)}, f32[768]{0:T(1024)}, u32[]{:S(2)}) copy-start(f32[768]{0:T(1024)} %get-tuple-element.84) | copy-start | bytes 9220
  (43 other events, 71.0 us)
Sparse Core Ops, SparseCore 0:
  51.6 35.4 reduce-scatter.15
  142.3 35.6 reduce-scatter.19
  180.4 22.2 reduce-scatter.17
  232.7 34.5 reduce-scatter.21
  270.2 33.9 reduce-scatter.31
  307.5 40.2 reduce-scatter.29
  350.2 48.0 reduce-scatter.27
  402.5 42.1 reduce-scatter.25
  448.6 42.4 reduce-scatter.23
